TPU v7x, 256 devices: a whole 4x4x8 slice. The times are simulated.
256 devices in a mesh: tok: 8 (over x, core), vocab: 32 (over z, y).
Axes of the slice: x: 4, y: 4, z: 8, core: 2. Of those that a mesh axis runs over, the one named last changes fastest.
Arguments:
- policy_hidden: bfloat16 [512, 5120], P(('tok', 'vocab')), may hold values from -15 to 15
- reference_hidden: bfloat16 [512, 5120], P(('tok', 'vocab')), may hold values from -15 to 15
- head_weight: bfloat16 [5120, 131072], P(None, ('tok', 'vocab')), may hold values from -1.118034 to 1.118034
- pair_map: int32 [512], replicated, may hold values from 0 to 511, each once
- response_mask: int32 [512], P(('tok', 'vocab')), may hold values 0 or 1
Outputs:
- token_divergence: float32 [512], P(('tok', 'vocab'))
- hidden_grad: bfloat16 [512, 5120], P(('tok', 'vocab'))
Inputs may be any that keep to these rules, and one draw needn't show every extreme that they name: pair_map is a permutation of the 512 rows.
All inputs are finite; a program needn't handle non-finite values. No bound on the sum of `response_mask` on one device may be relied on, other than what follows from the above.
Results may differ from a plain program's by a relative error of at most 0.015.
Values may be sent and summed in bfloat16 or wider, within the bound.
No kernel may reach another device: no remote copies, remote signals or barrier semaphores. Data moves between devices by JAX's collectives and lax.ppermute only.
A program may use at most 128 MiB of HBM per device.

v0:
```python
import jax
import jax.numpy as jnp
from jax import lax
from jax.sharding import PartitionSpec as P


def on_device(policy_hidden, reference_hidden, head_weight, pair_map, response_mask):
    own_rows = policy_hidden.shape[0]
    stacked = jnp.stack([policy_hidden, reference_hidden])
    logits = jnp.einsum(
        "srd,dv->srv",
        lax.all_gather(stacked, ("tok", "vocab"), axis=1, tiled=True),
        head_weight,
        preferred_element_type=jnp.float32,
    )
    policy_logits = logits[0]
    reference_logits = jnp.take(logits[1], pair_map, axis=0)
    difference = policy_logits - reference_logits
    policy_peak, reference_peak = lax.pmax(
        (jnp.max(policy_logits, axis=1), jnp.max(reference_logits, axis=1)), ("tok", "vocab")
    )
    policy_exp = jnp.exp(policy_logits - policy_peak[:, None])
    reference_exp = jnp.exp(reference_logits - reference_peak[:, None])
    policy_total, reference_total, weighted_sum = lax.psum(
        (
            jnp.sum(policy_exp, axis=1),
            jnp.sum(reference_exp, axis=1),
            jnp.sum(policy_exp * difference, axis=1),
        ),
        ("tok", "vocab"),
    )
    policy_lognorm = policy_peak + jnp.log(policy_total)
    reference_lognorm = reference_peak + jnp.log(reference_total)
    divergence = weighted_sum / policy_total - policy_lognorm + reference_lognorm
    log_ratio = difference - (policy_lognorm - reference_lognorm)[:, None]
    token_probs = jnp.exp(policy_logits - policy_lognorm[:, None])
    logit_grad = (token_probs * (log_ratio - divergence[:, None])).astype(jnp.bfloat16)
    grad_share = lax.psum_scatter(
        lax.dot_general(
            logit_grad, head_weight, (((1,), (1,)), ((), ())), preferred_element_type=jnp.float32
        ),
        ("tok", "vocab"),
        scatter_dimension=0,
        tiled=True,
    )
    position = (lax.axis_index("tok") * lax.axis_size("vocab") + lax.axis_index("vocab")) * own_rows
    own_divergence = lax.dynamic_slice_in_dim(divergence, position, own_rows, 0)
    weight = response_mask.astype(jnp.float32)
    return (weight * own_divergence, (weight[:, None] * grad_share).astype(jnp.bfloat16))


def solution(mesh):
    return jax.shard_map(
        on_device,
        mesh=mesh,
        in_specs=(
            P(("tok", "vocab"), None),
            P(("tok", "vocab"), None),
            P(None, ("tok", "vocab")),
            P(),
            P(("tok", "vocab")),
        ),
        out_specs=(P(("tok", "vocab")), P(("tok", "vocab"), None)),
        check_vma=False,
    )
```

profile of v0, /device:TPU:1, one launch (start us, length us, event | category | flops | bytes accessed | tf_op | source)
XLA Modules:
  0.0 596.6 jit_solution(1403346432027446092)
XLA Ops:
  7.2 0.0 all-gather.2.cloned.1.call-start
  7.2 0.8 pad_maximum_fusion
  8.0 0.6 copy.14
  8.7 0.0 all-gather.2.cloned.1.call-update
  8.7 0.0 all-reduce.5.cloned.1.call-start
  8.7 0.7 compare_select_fusion
  9.4 0.7 compare_and_fusion
  10.1 125.2 %all-gather.2.cloned.1.call-done = bf16[2,512,5120]{2,0,1:T(2,128)(2,1)} async-done(((bf16[2,2,5120]{2,0,1:T(2,128)(2,1)}), bf16[2,512,5120]{2,0,1:T(2,128)(2,1)}) %all-gather.2.cloned.1.call-update) | async-done | bytes 10485776 | tf_op jit(solution)/shard_map/all_gather | solution.py:12
  135.3 10.7 %fusion = f32[2,512,512]{1,2,0:T(8,128)S(1)} fusion(bf16[2,512,5120]{2,0,1:T(2,128)(2,1)} %all-gather.2.cloned.1.call-done, bf16[5120,512]{1,0:T(8,128)(2,1)} %param.7), kind=kOutput, calls=%fused_computation.1 | convolution fusion | flops 5368709120 | bytes 17825792 | tf_op jit(solution)/shard_map/srd,dv->srv/dot_general | solution.py:10
  146.0 1.1 slice_bitcast_fusion
  147.2 1.6 copy.17
  148.7 2.3 gather_fusion
  151.1 1.6 copy.18
  152.6 0.2 select_reduce_fusion
  152.8 74.6 %all-reduce.2 = (f32[512]{0:T(512)S(1)}, f32[512]{0:T(512)S(1)}) all-reduce(f32[512]{0:T(512)S(1)} %get-tuple-element.13, f32[512]{0:T(512)S(1)} %select_reduce_fusion), channel_id=1, replica_groups=mesh['tok'=8,'vocab'=32] {'tok','vocab'}, use_global_device_ids=true, to_apply=%region_1.2 | all-reduce | flops 1024 | bytes 8192 | tf_op jit(solution)/shard_map/pmax | solution.py:19
  227.4 0.4 multiply_reduce_fusion
  227.8 73.5 %all-reduce.1 = (f32[512]{0:T(512)S(1)}, f32[512]{0:T(512)S(1)}, f32[512]{0:T(512)S(1)}) all-reduce(f32[512]{0:T(512)S(1)} %get-tuple-element.3, f32[512]{0:T(512)S(1)} %get-tuple-element.2, f32[512]{0:T(512)S(1)} %get-tuple-element.4), channel_id=1, replica_groups=mesh['tok'=8,'vocab'=32] {'tok','vocab'}, use_global_device_ids=true, to_apply=%region_5.6 | all-reduce | flops 1536 | bytes 12288 | tf_op jit(solution)/shard_map/psum | solution.py:24
  301.3 8.0 %fusion.8 = f32[512,5120]{1,0:T(8,128)} fusion(bf16[5120,512]{1,0:T(8,128)(2,1)} %param.7, f32[512,512]{0,1:T(8,128)S(1)} %copy.18, f32[2,512,512]{1,2,0:T(8,128)S(1)} %fusion, f32[512]{0:T(512)S(1)} %subtract_add_fusion, f32[512]{0:T(512)S(1)} %get-tuple-element.10, f32[512]{0:T(512)S(1)} %get-tuple-element.11, pred[512]{0:T(512)(128)(4,1)S(1)} %compare_and_fusion), kind=kOutput, calls=%fused_computation.17 | convolution fusion | flops 2686189568 | bytes 17832448 | tf_op jit(solution)/shard_map/dot_general | solution.py:39
  309.3 0.0 copy-start
  309.3 0.0 all-reduce.5.cloned.1.call-update
  309.3 0.6 copy-done
  310.0 0.6 dynamic-slice_multiply_fusion.1
  310.5 277.6 %all-reduce.5.cloned.1.call-done = f32[512,5120]{1,0:T(8,128)} async-done(((f32[512,5120]{1,0:T(8,128)}), f32[512,5120]{1,0:T(8,128)}) %all-reduce.5.cloned.1.call-update) | async-done | bytes 10485776
  588.1 1.6 fusion.15
  (4 shorter events, 0.0 us)
Async XLA Ops:
  7.2 128.2 %all-gather.2.cloned.1.call-start = ((), (), s32[]{:S(2)}) async-start(), calls=%async_computation | async-start | bytes 10526720 | tf_op jit(solution)/shard_map/all_gather | solution.py:12
  8.7 579.4 %all-reduce.5.cloned.1.call-start = ((), (), s32[]{:S(2)}) async-start(), calls=%async_computation.1 | async-start | bytes 20971520
  309.3 0.7 copy-start
Sparse Core Ops, SparseCore 0:
  11.6 123.6 all-gather.1
  309.5 278.6 all-reduce.4
where the time goes:
time: 598 us; the launch traced here: 597 us
  waiting for transfers between devices  403 us (67%)
  blocking collectives  148 us (25%)
  matrix products  18.7 us (3%)
  between operations  14.1 us (2%)
  local copies, waits for them, and re-layouts  6.72 us (1%)
  other arithmetic  6.1 us (1%)
    unnamed x3, waiting for transfers between devices  278 us
    all_gather x1, waiting for transfers between devices, on_device(): lax.all_gather(stacked, ('tok', 'vocab'), axis=1, tiled=True)  125 us
    pmax x1, blocking collectives, on_device(): lax.pmax((jnp.max(policy_logits, axis=1), jnp.max(reference_logits, axis=...  74.6 us
    psum x1, blocking collectives, on_device(): lax.psum((jnp.sum(policy_exp, axis=1), jnp.sum(reference_exp, axis=1), jn...  73.5 us
  transfers between devices with their start and end apart: 2, of which 2 were waited for; matrix products, arithmetic and copies ran while one was open for 0% of the time, Pallas kernels for 0%

commit v1 on v0

v1 whole, which is shorter than its diff:
```python
import jax
import jax.numpy as jnp
from jax import lax
from jax.sharding import PartitionSpec as P

X, CORES, Z, Y = 4, 2, 8, 4
F32, BF16 = jnp.float32, jnp.bfloat16


def flat(x, c, z, y):
    return ((x * CORES + c) * Z + z) * Y + y


def exchange(value, partner):
    pairs = [
        (flat(x, c, z, y), flat(*partner(x, c, z, y)))
        for x in range(X)
        for c in range(CORES)
        for z in range(Z)
        for y in range(Y)
    ]
    return lax.ppermute(value, ("tok", "vocab"), pairs)


def along_x(first, second):
    return lambda x, c, z, y: (x ^ (second if c else first), c, z, y)


def along_y(first, second):
    return lambda x, c, z, y: (x, c, z, y ^ (second if c else first))


def along_z(step):
    return lambda x, c, z, y: (x, c, z ^ step, y)


def across_cores(x, c, z, y):
    return (x, 1 - c, z, y)


Z_STEPS = (1, 2, 6)


def gray(j):
    return j ^ (j >> 1)


def z_slot(j):
    return j ^ ((j >> 2) << 1)


def gather_z(rows):
    for step in Z_STEPS:
        rows = jnp.concatenate([rows, exchange(rows, along_z(step))], 0)
    return rows


def gather_ring(rows, along, second_core):
    count = rows.shape[0]
    near = exchange(rows, along(1, 3))
    far = exchange(jnp.concatenate([rows, near], 0), along(3, 1))
    return jnp.concatenate(
        [
            rows,
            jnp.where(second_core, far[:count], near),
            jnp.where(second_core, near, far[:count]),
            far[count:],
        ],
        0,
    )


def scatter_step(total, partner):
    half = total.shape[0] // 2
    return total[:half] + exchange(total[half:].astype(BF16), partner).astype(F32)


def merge(a, b):
    policy_peak = jnp.maximum(a[0], b[0])
    reference_peak = jnp.maximum(a[1], b[1])
    pa, pb = jnp.exp(a[0] - policy_peak), jnp.exp(b[0] - policy_peak)
    ra, rb = jnp.exp(a[1] - reference_peak), jnp.exp(b[1] - reference_peak)
    return jnp.stack(
        [
            policy_peak,
            reference_peak,
            a[2] * pa + b[2] * pb,
            a[3] * ra + b[3] * rb,
            a[4] * pa + b[4] * pb,
        ]
    )


def on_device(policy_hidden, reference_hidden, head_weight, pair_map, response_mask):
    tok, vocab = lax.axis_index("tok"), lax.axis_index("vocab")
    x0, c0, z0, y0 = tok // CORES, tok % CORES, vocab // Y, vocab % Y
    second = c0 == 1
    own_rows, width = policy_hidden.shape
    half = width // 2
    columns = head_weight.shape[1]
    chip_rows = CORES * own_rows
    tokens = X * Y * Z * chip_rows
    mine = tokens // 2

    own = jnp.concatenate([policy_hidden, reference_hidden], 0)
    keep = lax.dynamic_slice_in_dim(own, c0 * half, half, 1)
    got = exchange(lax.dynamic_slice_in_dim(own, (1 - c0) * half, half, 1), across_cores)
    first_rows = jnp.where(second, got, keep)
    second_rows = jnp.where(second, keep, got)
    rows = jnp.concatenate(
        [first_rows[:own_rows], second_rows[:own_rows], first_rows[own_rows:], second_rows[own_rows:]], 0
    )
    head_keep = lax.dynamic_slice_in_dim(head_weight, c0 * half, half, 0)
    head_got = exchange(lax.dynamic_slice_in_dim(head_weight, (1 - c0) * half, half, 0), across_cores)
    head = jnp.concatenate([head_keep, head_got], 1)

    rows = gather_z(rows).reshape(Z, 2, chip_rows, half)
    policy = rows[:, 0].reshape(Z * chip_rows, half)
    paired = rows[:, 1].reshape(Z * chip_rows, half)
    policy = gather_ring(policy, along_x, second)
    paired = gather_ring(paired, along_y, second)
    policy = gather_ring(policy, along_y, second)
    paired = gather_ring(paired, along_x, second)

    slot = jnp.arange(tokens, dtype=jnp.int32)
    sr, sc = slot % own_rows, (slot // own_rows) % CORES
    sz = z_slot((slot // chip_rows) % Z) ^ z0
    sx = gray((slot // (chip_rows * Z)) % X) ^ x0
    sy = gray(slot // (chip_rows * Z * X)) ^ y0
    partner = jnp.take(pair_map, flat(sx, sc, sz, sy) * own_rows + sr, axis=0)
    pr, pdev = partner % own_rows, partner // own_rows
    py, pz, pc, px = pdev % Y, (pdev // Y) % Z, (pdev // (Y * Z)) % CORES, pdev // (Y * Z * CORES)
    place = (((gray(px ^ x0) * Y + gray(py ^ y0)) * Z + z_slot(pz ^ z0)) * CORES + pc) * own_rows + pr
    one_hot = (place[:, None] == jnp.arange(tokens, dtype=jnp.int32)[None]).astype(BF16)
    paired = jnp.dot(one_hot, paired, preferred_element_type=F32).astype(BF16)

    policy_part = jnp.dot(policy, head, preferred_element_type=F32)
    reference_part = jnp.dot(paired, head, preferred_element_type=F32)

    def finish(part):
        keep = lax.dynamic_slice_in_dim(part, c0 * mine, mine, 0)
        send = lax.dynamic_slice_in_dim(part, (1 - c0) * mine, mine, 0)
        got = exchange(send, across_cores)
        return keep + jnp.concatenate([got[:, columns:], got[:, :columns]], 1)

    policy_logits = finish(policy_part)
    reference_logits = finish(reference_part)
    difference = policy_logits - reference_logits

    policy_peak = jnp.max(policy_logits, axis=1)
    reference_peak = jnp.max(reference_logits, axis=1)
    policy_exp = jnp.exp(policy_logits - policy_peak[:, None])
    reference_exp = jnp.exp(reference_logits - reference_peak[:, None])
    stats = jnp.stack(
        [
            policy_peak,
            reference_peak,
            jnp.sum(policy_exp, axis=1),
            jnp.sum(reference_exp, axis=1),
            jnp.sum(policy_exp * difference, axis=1),
        ]
    )
    order = (5, 2, 2, 2, 2, 2, 2, chip_rows)
    for partner_of, bit in (
        (along_z(1), 6),
        (along_z(2), 5),
        (along_z(6), 4),
        (along_x(1, 1), 3),
        (along_x(3, 3), 2),
        (along_y(1, 1), 1),
        (lambda x, c, z, y: (x, 1 - c, z, y ^ 3), None),
    ):
        other = exchange(stats, partner_of)
        if bit is not None:
            other = jnp.flip(other.reshape(order), bit).reshape(stats.shape)
        stats = merge(stats, other)
    policy_peak, reference_peak, policy_total, reference_total, weighted_sum = stats

    policy_lognorm = policy_peak + jnp.log(policy_total)
    reference_lognorm = reference_peak + jnp.log(reference_total)
    divergence = weighted_sum / policy_total - policy_lognorm + reference_lognorm
    log_ratio = difference - (policy_lognorm - reference_lognorm)[:, None]
    token_probs = jnp.exp(policy_logits - policy_lognorm[:, None])
    logit_grad = (token_probs * (log_ratio - divergence[:, None])).astype(BF16)

    got = exchange(jnp.concatenate([logit_grad[:, columns:], logit_grad[:, :columns]], 1), across_cores)
    quarter = mine // 2
    m0, m1, g0, g1 = logit_grad[:quarter], logit_grad[quarter:], got[:quarter], got[quarter:]
    by_y = jnp.stack(
        [jnp.where(second, g0, m0), jnp.where(second, m0, m1), jnp.where(second, g1, g0), jnp.where(second, m1, g1)]
    ).reshape(Y, X, Z * chip_rows, 2 * columns)
    by_y = jnp.stack(
        [
            by_y[:, 0],
            jnp.where(second, by_y[:, 2], by_y[:, 1]),
            jnp.where(second, by_y[:, 1], by_y[:, 2]),
            by_y[:, 3],
        ],
        1,
    )
    by_x = jnp.swapaxes(by_y, 0, 1).reshape(tokens, 2 * columns)
    by_y = by_y.reshape(tokens, 2 * columns)

    def share(grad, weights):
        return lax.dot_general(grad, weights, (((1,), (1,)), ((), ())), preferred_element_type=F32)

    def first_step(grad, weights, partner):
        sent = exchange(share(grad[mine:], weights).astype(BF16), partner)
        return share(grad[:mine], weights) + sent.astype(F32)

    low, high = head[: half // 2], head[half // 2 :]
    low_total = first_step(by_y, low, along_y(3, 1))
    high_total = first_step(by_x, high, along_x(3, 1))
    low_total = scatter_step(low_total, along_y(1, 3))
    high_total = scatter_step(high_total, along_x(1, 3))
    low_total = scatter_step(scatter_step(low_total, along_x(3, 1)), along_x(1, 3))
    high_total = scatter_step(scatter_step(high_total, along_y(3, 1)), along_y(1, 3))
    total = jnp.concatenate([low_total, high_total], 1)
    for step in Z_STEPS[::-1]:
        total = scatter_step(total, along_z(step))

    keep = lax.dynamic_slice_in_dim(total, c0 * own_rows, own_rows, 0)
    got = exchange(lax.dynamic_slice_in_dim(total, (1 - c0) * own_rows, own_rows, 0), across_cores)
    grad = jnp.concatenate([jnp.where(second, got, keep), jnp.where(second, keep, got)], 1)
    other_divergence = exchange(divergence[:chip_rows], across_cores)
    own_divergence = jnp.where(second, other_divergence[own_rows:chip_rows], divergence[:own_rows])
    weight = response_mask.astype(F32)
    return (weight * own_divergence, (weight[:, None] * grad).astype(BF16))


def solution(mesh):
    return jax.shard_map(
        on_device,
        mesh=mesh,
        in_specs=(
            P(("tok", "vocab"), None),
            P(("tok", "vocab"), None),
            P(None, ("tok", "vocab")),
            P(),
            P(("tok", "vocab")),
        ),
        out_specs=(P(("tok", "vocab")), P(("tok", "vocab"), None)),
        check_vma=False,
    )
```

time: 598 us -> 234 us (0.39)
  waiting for transfers between devices: 403 us -> 66 us
  blocking collectives: 148 us -> 0 us
  starting transfers between devices: 0.08 us -> 84.6 us
  local copies, waits for them, and re-layouts: 6.72 us -> 39.2 us
  between operations: 14.1 us -> 2.19 us
  other arithmetic: 6.1 us -> 14.4 us
    unnamed x3 -> x0, waiting for transfers between devices: 278 us -> none
    all_gather x1 -> x0, waiting for transfers between devices: 125 us -> none  [on_device(): lax.all_gather(stacked, ('tok', 'vocab'), axis=1, tiled=True)]
    ppermute x0 -> x36, starting transfers between devices: none -> 84.6 us  [exchange(): return lax.ppermute(value, ('tok', 'vocab'), pairs)]
    pmax x1 -> x0, blocking collectives: 74.6 us -> none  [on_device(): lax.pmax((jnp.max(policy_logits, axis=1), jnp.max(reference_logits, axis=...]
    psum x1 -> x0, blocking collectives: 73.5 us -> none  [on_device(): lax.psum((jnp.sum(policy_exp, axis=1), jnp.sum(reference_exp, axis=1), jn...]
    ppermute x0 -> x36, waiting for transfers between devices: none -> 66 us  [exchange(): return lax.ppermute(value, ('tok', 'vocab'), pairs)]
    dynamic_slice x0 -> x4, local copies, waits for them, and re-layouts: none -> 8.97 us  [the longest x1 5.22 us: on_device(): head_keep = lax.dynamic_slice_in_dim(head_weight, c0 * half, half, 0)]
    unnamed x0 -> x7, other arithmetic: none -> 8.56 us
  transfers between devices with their start and end apart: 2 -> 36, of which waited for: 2 -> 27; matrix products, arithmetic and copies ran while one was open for 0% -> 23% of each run, Pallas kernels for 0% -> 0%
where the time goes in v1:
time: 234 us; the launch traced here: 230 us
  starting transfers between devices  84.6 us (36%)
  waiting for transfers between devices  66 us (28%)
  local copies, waits for them, and re-layouts  39.2 us (17%)
  matrix products  23.2 us (10%)
  other arithmetic  14.4 us (6%)
    ppermute x36, starting transfers between devices, exchange(): return lax.ppermute(value, ('tok', 'vocab'), pairs)  84.6 us
    ppermute x36, waiting for transfers between devices, exchange(): return lax.ppermute(value, ('tok', 'vocab'), pairs)  66 us
    dot_general x1, matrix products, on_device(): reference_part = jnp.dot(paired, head, preferred_element_type=F32)  8.89 us
    dot_general x4, matrix products, share(): lax.dot_general(grad, weights, (((1,), (1,)), ((), ())), preferred_elemen...  8.86 us
    unnamed x7, other arithmetic  8.56 us
    unnamed x24, local copies, waits for them, and re-layouts  7.19 us
    dot_general x1, matrix products, on_device(): policy_part = jnp.dot(policy, head, preferred_element_type=F32)  5.4 us
    dynamic_slice x1, local copies, waits for them, and re-layouts, on_device(): head_keep = lax.dynamic_slice_in_dim(head_weight, c0 * half, half, 0)  5.22 us
  transfers between devices with their start and end apart: 36, of which 27 were waited for; matrix products, arithmetic and copies ran while one was open for 23% of the time, Pallas kernels for 0%

profile of v1, /device:TPU:1, one launch (start us, length us, event | category | flops | bytes accessed | tf_op | source)
XLA Modules:
  0.0 229.6 jit_solution(1797079343372534710)
XLA Ops:
  1.5 3.3 %collective-permute-start = (bf16[4,2560]{1,0:T(4,128)(2,1)S(1)}, bf16[4,2560]{1,0:T(4,128)(2,1)S(1)}, u32[]{:S(2)}, u32[]{:S(2)}) collective-permute-start(bf16[4,2560]{1,0:T(4,128)(2,1)S(1)} %fusion.11), channel_id=1, source_target_pairs={{0,32},{1,33},{2,34},{3,35},{4,36},{5,37},{6,38},{7,39},{8,40},{9,... | collective-permute-start | bytes 61448 | tf_op jit(solution)/shard_map/ppermute | solution.py:22
  6.8 2.8 %collective-permute-done.1 = bf16[8,2560]{1,0:T(8,128)(2,1)S(1)} collective-permute-done((bf16[8,2560]{1,0:T(8,128)(2,1)S(1)}, bf16[8,2560]{1,0:T(8,128)(2,1)S(1)}, u32[]{:S(2)}, u32[]{:S(2)}) %collective-permute-start.1) | collective-permute-done | bytes 40992 | tf_op jit(solution)/shard_map/ppermute | solution.py:22
  11.2 3.6 %collective-permute-done.2 = bf16[16,2560]{1,0:T(8,128)(2,1)S(1)} collective-permute-done((bf16[16,2560]{1,0:T(8,128)(2,1)S(1)}, bf16[16,2560]{1,0:T(8,128)(2,1)S(1)}, u32[]{:S(2)}, u32[]{:S(2)}) %collective-permute-start.2) | collective-permute-done | bytes 81952 | tf_op jit(solution)/shard_map/ppermute | solution.py:22
  14.9 3.6 %collective-permute-start.3 = (bf16[32,2560]{1,0:T(8,128)(2,1)S(1)}, bf16[32,2560]{1,0:T(8,128)(2,1)S(1)}, u32[]{:S(2)}, u32[]{:S(2)}) collective-permute-start(bf16[32,2560]{1,0:T(8,128)(2,1)S(1)} %concatenate.68), channel_id=1, source_target_pairs={{0,24},{1,25},{2,26},{3,27},{4,28},{5,29},{6,30},{7,31},{8,16},{9,... | collective-permute-start | bytes 491528 | tf_op jit(solution)/shard_map/ppermute | solution.py:22
  18.5 4.2 %collective-permute-done.3 = bf16[32,2560]{1,0:T(8,128)(2,1)S(1)} collective-permute-done((bf16[32,2560]{1,0:T(8,128)(2,1)S(1)}, bf16[32,2560]{1,0:T(8,128)(2,1)S(1)}, u32[]{:S(2)}, u32[]{:S(2)}) %collective-permute-start.3) | collective-permute-done | bytes 163872 | tf_op jit(solution)/shard_map/ppermute | solution.py:22
  26.5 2.8 %collective-permute-start.10 = (bf16[32,2560]{1,0:T(8,128)(2,1)S(1)}, bf16[32,2560]{1,0:T(8,128)(2,1)S(1)}, u32[]{:S(2)}, u32[]{:S(2)}) collective-permute-start(bf16[32,2560]{1,0:T(8,128)(2,1)S(1)} %reshape_squeeze.7), channel_id=1, source_target_pairs={{0,1},{1,0},{2,3},{3,2},{4,5},{5,4},{6,7},{7,6},{8,9},{9,8},{10,11... | collective-permute-start | bytes 491528 | tf_op jit(solution)/shard_map/ppermute | solution.py:22
  32.5 3.7 %collective-permute-done.5 = bf16[64,2560]{1,0:T(8,128)(2,1)S(1)} collective-permute-done((bf16[64,2560]{1,0:T(8,128)(2,1)S(1)}, bf16[64,2560]{1,0:T(8,128)(2,1)S(1)}, u32[]{:S(2)}, u32[]{:S(2)}) %collective-permute-start.5) | collective-permute-done | bytes 327712 | tf_op jit(solution)/shard_map/ppermute | solution.py:22
  51.6 4.2 %collective-permute-done.12 = bf16[128,2560]{1,0:T(8,128)(2,1)S(1)} collective-permute-done((bf16[128,2560]{1,0:T(8,128)(2,1)S(1)}, bf16[128,2560]{1,0:T(8,128)(2,1)S(1)}, u32[]{:S(2)}, u32[]{:S(2)}) %collective-permute-start.12) | collective-permute-done | bytes 655392 | tf_op jit(solution)/shard_map/ppermute | solution.py:22
  57.0 5.2 %constant_dynamic-slice_fusion.4 = (bf16[2560,512]{1,0:T(8,128)(2,1)}, bf16[2560,512]{1,0:T(8,128)(2,1)}) fusion(bf16[5120,512]{1,0:T(8,128)(2,1)} %param.7, s32[]{:T(128)S(6)} %select_n.380, s32[]{:T(128)S(6)} %select_n.379), kind=kLoop, calls=%fused_computation.183 | loop fusion | bytes 10485768 | tf_op jit(solution)/shard_map/dynamic_slice | solution.py:113
  62.2 7.7 %collective-permute-start.8 = (bf16[2560,512]{1,0:T(8,128)(2,1)}, bf16[2560,512]{1,0:T(8,128)(2,1)}, u32[]{:S(2)}, u32[]{:S(2)}) collective-permute-start(bf16[2560,512]{1,0:T(8,128)(2,1)} %get-tuple-element.75), channel_id=1, source_target_pairs={{0,32},{1,33},{2,34},{3,35},{4,36},{5,37},{6,38},{7,39},{8,40},{9,... | collective-permute-start | bytes 7864328 | tf_op jit(solution)/shard_map/ppermute | solution.py:22
  70.0 3.5 %gather_fusion = s32[512]{0:T(512)S(1)} fusion(s32[512]{0:T(512)S(1)} %copy-done, s32[1024]{0:T(1024)S(1)} %pad_clamp_fusion), kind=kCustom, calls=%fused_computation | custom fusion | bytes 6144 | tf_op jit(solution)/shard_map/jit(_take)/gather | solution.py:130
  81.3 5.4 %fusion.1 = f32[512,1024]{1,0:T(8,128)S(1)} fusion(bf16[512,2560]{1,0:T(8,128)(2,1)} %slice_dynamic-update-slice_fusion.1, bf16[2560,512]{1,0:T(8,128)(2,1)} %collective-permute-done.8, bf16[2560,512]{1,0:T(8,128)(2,1)S(1)} %copy-done.2), kind=kOutput, calls=%fused_computation.8 | convolution fusion | flops 2694840320 | bytes 9961472 | tf_op jit(solution)/shard_map/dot_general | solution.py:137
  87.9 7.1 %collective-permute-start.9 = (f32[256,1024]{1,0:T(8,128)}, f32[256,1024]{1,0:T(8,128)}, u32[]{:S(2)}, u32[]{:S(2)}) collective-permute-start(f32[256,1024]{1,0:T(8,128)} %constant_dynamic-slice_fusion.2), channel_id=1, source_target_pairs={{0,32},{1,33},{2,34},{3,35},{4,36},{5,37},{6,38},{7,39},{8,40},{9,... | collective-permute-start | bytes 3145736 | tf_op jit(solution)/shard_map/ppermute | solution.py:22
  96.9 8.9 %fusion = f32[512,1024]{1,0:T(8,128)} fusion(bf16[2560,512]{1,0:T(8,128)(2,1)} %collective-permute-done.8, bf16[2560,512]{1,0:T(8,128)(2,1)} %get-tuple-element.74, bf16[512,2560]{1,0:T(8,128)(2,1)} %slice_dynamic-update-slice_fusion, s32[512]{0:T(512)S(1)} %fusion.45), kind=kOutput, calls=%fused_computation.7 | convolution fusion | flops 4038590464 | bytes 9963520 | tf_op jit(solution)/shard_map/dot_general | solution.py:138
  122.8 4.0 %collective-permute-start.17 = (f32[5,256]{1,0:T(8,128)S(1)}, f32[5,256]{1,0:T(8,128)S(1)}, u32[]{:S(2)}, u32[]{:S(2)}) collective-permute-start(f32[5,256]{1,0:T(8,128)S(1)} %stack.43), channel_id=1, source_target_pairs={{0,24},{1,25},{2,26},{3,27},{4,28},{5,29},{6,30},{7,31},{8,16},{9,... | collective-permute-start | bytes 15368 | tf_op jit(solution)/shard_map/ppermute | solution.py:22
  138.4 8.9 %collective-permute-start.20 = (f32[5,256]{1,0:T(8,128)S(1)}, f32[5,256]{1,0:T(8,128)S(1)}, u32[]{:S(2)}, u32[]{:S(2)}) collective-permute-start(f32[5,256]{1,0:T(8,128)S(1)} %stack.46), channel_id=1, source_target_pairs={{0,1},{1,0},{2,3},{3,2},{4,5},{5,4},{6,7},{7,6},{8,9},{9,8},{10,11... | collective-permute-start | bytes 15368 | tf_op jit(solution)/shard_map/ppermute | solution.py:22
  151.2 10.2 %collective-permute-start.21 = (f32[5,256]{1,0:T(8,128)S(1)}, f32[5,256]{1,0:T(8,128)S(1)}, u32[]{:S(2)}, u32[]{:S(2)}) collective-permute-start(f32[5,256]{1,0:T(8,128)S(1)} %stack.47), channel_id=1, source_target_pairs={{0,35},{1,34},{2,33},{3,32},{4,39},{5,38},{6,37},{7,36},{8,43},{9,... | collective-permute-start | bytes 15368 | tf_op jit(solution)/shard_map/ppermute | solution.py:22
  175.4 6.1 %collective-permute-done.28 = bf16[256,1280]{1,0:T(8,128)(2,1)S(1)} collective-permute-done((bf16[256,1280]{1,0:T(8,128)(2,1)S(1)}, bf16[256,1280]{1,0:T(8,128)(2,1)S(1)}, u32[]{:S(2)}, u32[]{:S(2)}) %collective-permute-start.28) | collective-permute-done | bytes 655392 | tf_op jit(solution)/shard_map/ppermute | solution.py:22
  192.4 3.4 %collective-permute-done.25 = bf16[128,1280]{1,0:T(8,128)(2,1)S(1)} collective-permute-done((bf16[128,1280]{1,0:T(8,128)(2,1)S(1)}, bf16[128,1280]{1,0:T(8,128)(2,1)S(1)}, u32[]{:S(2)}, u32[]{:S(2)}) %collective-permute-start.25) | collective-permute-done | bytes 327712 | tf_op jit(solution)/shard_map/ppermute | solution.py:22
  202.1 3.8 %collective-permute-done.27 = bf16[32,1280]{1,0:T(8,128)(2,1)S(1)} collective-permute-done((bf16[32,1280]{1,0:T(8,128)(2,1)S(1)}, bf16[32,1280]{1,0:T(8,128)(2,1)S(1)}, u32[]{:S(2)}, u32[]{:S(2)}) %collective-permute-start.27) | collective-permute-done | bytes 81952 | tf_op jit(solution)/shard_map/ppermute | solution.py:22
  205.9 4.0 %collective-permute-start.32 = (bf16[16,2560]{1,0:T(8,128)(2,1)S(1)}, bf16[16,2560]{1,0:T(8,128)(2,1)S(1)}, u32[]{:S(2)}, u32[]{:S(2)}) collective-permute-start(bf16[16,2560]{1,0:T(8,128)(2,1)S(1)} %fusion.8), channel_id=1, source_target_pairs={{0,24},{1,25},{2,26},{3,27},{4,28},{5,29},{6,30},{7,31},{8,16},{9,... | collective-permute-start | bytes 245768 | tf_op jit(solution)/shard_map/ppermute | solution.py:22
  212.3 3.8 %collective-permute-done.33 = bf16[8,2560]{1,0:T(8,128)(2,1)S(1)} collective-permute-done((bf16[8,2560]{1,0:T(8,128)(2,1)S(1)}, bf16[8,2560]{1,0:T(8,128)(2,1)S(1)}, u32[]{:S(2)}, u32[]{:S(2)}) %collective-permute-start.33) | collective-permute-done | bytes 40992 | tf_op jit(solution)/shard_map/ppermute | solution.py:22
  216.3 7.8 %collective-permute-start.22 = (f32[4]{0:T(128)S(1)}, f32[4]{0:T(128)S(1)}, u32[]{:S(2)}, u32[]{:S(2)}) collective-permute-start(f32[4]{0:T(128)S(1)} %slice.634), channel_id=1, source_target_pairs={{0,32},{1,33},{2,34},{3,35},{4,36},{5,37},{6,38},{7,39},{8,40},{9,... | collective-permute-start | bytes 56 | tf_op jit(solution)/shard_map/ppermute | solution.py:22
  224.1 3.7 %collective-permute-start.35 = (f32[2,2560]{1,0:T(2,128)S(1)}, f32[2,2560]{1,0:T(2,128)S(1)}, u32[]{:S(2)}, u32[]{:S(2)}) collective-permute-start(f32[2,2560]{1,0:T(2,128)S(1)} %constant_dynamic-slice_fusion), channel_id=1, source_target_pairs={{0,32},{1,33},{2,34},{3,35},{4,36},{5,37},{6,38},{7,39},{8,40},{9,... | collective-permute-start | bytes 61448 | tf_op jit(solution)/shard_map/ppermute | solution.py:22
  (307 shorter events, 105.6 us)
Async XLA Ops:
  9.7 5.2 %collective-permute-start.2 = (bf16[16,2560]{1,0:T(8,128)(2,1)S(1)}, bf16[16,2560]{1,0:T(8,128)(2,1)S(1)}, u32[]{:S(2)}, u32[]{:S(2)}) collective-permute-start(bf16[16,2560]{1,0:T(8,128)(2,1)S(1)} %concatenate.67), channel_id=1, source_target_pairs={{0,8},{1,9},{2,10},{3,11},{4,12},{5,13},{6,14},{7,15},{8,0},{9,1},... | collective-permute-start | bytes 245768 | tf_op jit(solution)/shard_map/ppermute | solution.py:22
  14.9 7.8 %collective-permute-start.3 = (bf16[32,2560]{1,0:T(8,128)(2,1)S(1)}, bf16[32,2560]{1,0:T(8,128)(2,1)S(1)}, u32[]{:S(2)}, u32[]{:S(2)}) collective-permute-start(bf16[32,2560]{1,0:T(8,128)(2,1)S(1)} %concatenate.68), channel_id=1, source_target_pairs={{0,24},{1,25},{2,26},{3,27},{4,28},{5,29},{6,30},{7,31},{8,16},{9,... | collective-permute-start | bytes 491528 | tf_op jit(solution)/shard_map/ppermute | solution.py:22
  23.1 7.0 %collective-permute-start.4 = (bf16[32,2560]{1,0:T(8,128)(2,1)S(1)}, bf16[32,2560]{1,0:T(8,128)(2,1)S(1)}, u32[]{:S(2)}, u32[]{:S(2)}) collective-permute-start(bf16[32,2560]{1,0:T(8,128)(2,1)S(1)} %reshape_squeeze.6), channel_id=1, source_target_pairs={{0,64},{1,65},{2,66},{3,67},{4,68},{5,69},{6,70},{7,71},{8,72},{9,... | collective-permute-start | bytes 491528 | tf_op jit(solution)/shard_map/ppermute | solution.py:22
  26.5 5.5 %collective-permute-start.10 = (bf16[32,2560]{1,0:T(8,128)(2,1)S(1)}, bf16[32,2560]{1,0:T(8,128)(2,1)S(1)}, u32[]{:S(2)}, u32[]{:S(2)}) collective-permute-start(bf16[32,2560]{1,0:T(8,128)(2,1)S(1)} %reshape_squeeze.7), channel_id=1, source_target_pairs={{0,1},{1,0},{2,3},{3,2},{4,5},{5,4},{6,7},{7,6},{8,9},{9,8},{10,11... | collective-permute-start | bytes 491528 | tf_op jit(solution)/shard_map/ppermute | solution.py:22
  30.1 6.0 %collective-permute-start.5 = (bf16[64,2560]{1,0:T(8,128)(2,1)S(1)}, bf16[64,2560]{1,0:T(8,128)(2,1)S(1)}, u32[]{:S(2)}, u32[]{:S(2)}) collective-permute-start(bf16[64,2560]{1,0:T(8,128)(2,1)S(1)} %pad_maximum_fusion.8), channel_id=1, source_target_pairs={{0,192},{1,193},{2,194},{3,195},{4,196},{5,197},{6,198},{7,199},{8... | collective-permute-start | bytes 983048 | tf_op jit(solution)/shard_map/ppermute | solution.py:22
  32.1 9.4 %collective-permute-start.11 = (bf16[64,2560]{1,0:T(8,128)(2,1)S(1)}, bf16[64,2560]{1,0:T(8,128)(2,1)S(1)}, u32[]{:S(2)}, u32[]{:S(2)}) collective-permute-start(bf16[64,2560]{1,0:T(8,128)(2,1)S(1)} %pad_maximum_fusion.9), channel_id=1, source_target_pairs={{0,3},{1,2},{2,1},{3,0},{4,7},{5,6},{6,5},{7,4},{8,11},{9,10},{10,... | collective-permute-start | bytes 983048 | tf_op jit(solution)/shard_map/ppermute | solution.py:22
  39.7 10.7 %collective-permute-start.6 = (bf16[128,2560]{1,0:T(8,128)(2,1)S(1)}, bf16[128,2560]{1,0:T(8,128)(2,1)S(1)}, u32[]{:S(2)}, u32[]{:S(2)}) collective-permute-start(bf16[128,2560]{1,0:T(8,128)(2,1)S(1)} %pad_maximum_fusion.5), channel_id=1, source_target_pairs={{0,1},{1,0},{2,3},{3,2},{4,5},{5,4},{6,7},{7,6},{8,9},{9,8},{10,11... | collective-permute-start | bytes 1966088 | tf_op jit(solution)/shard_map/ppermute | solution.py:22
  45.0 10.7 %collective-permute-start.12 = (bf16[128,2560]{1,0:T(8,128)(2,1)S(1)}, bf16[128,2560]{1,0:T(8,128)(2,1)S(1)}, u32[]{:S(2)}, u32[]{:S(2)}) collective-permute-start(bf16[128,2560]{1,0:T(8,128)(2,1)S(1)} %pad_maximum_fusion.6), channel_id=1, source_target_pairs={{0,64},{1,65},{2,66},{3,67},{4,68},{5,69},{6,70},{7,71},{8,72},{9,... | collective-permute-start | bytes 1966088 | tf_op jit(solution)/shard_map/ppermute | solution.py:22
  51.3 22.3 %collective-permute-start.7 = (bf16[256,2560]{1,0:T(8,128)(2,1)}, bf16[256,2560]{1,0:T(8,128)(2,1)}, u32[]{:S(2)}, u32[]{:S(2)}) collective-permute-start(bf16[256,2560]{1,0:T(8,128)(2,1)} %constant_dynamic-update-slice_fusion), channel_id=1, source_target_pairs={{0,3},{1,2},{2,1},{3,0},{4,7},{5,6},{6,5},{7,4},{8,11},{9,10},{10,... | collective-permute-start | bytes 3932168 | tf_op jit(solution)/shard_map/ppermute | solution.py:22
  56.6 17.9 %collective-permute-start.13 = (bf16[256,2560]{1,0:T(8,128)(2,1)}, bf16[256,2560]{1,0:T(8,128)(2,1)S(1)}, u32[]{:S(2)}, u32[]{:S(2)}) collective-permute-start(bf16[256,2560]{1,0:T(8,128)(2,1)} %constant_dynamic-update-slice_fusion.9), channel_id=1, source_target_pairs={{0,192},{1,193},{2,194},{3,195},{4,196},{5,197},{6,198},{7,199},{8... | collective-permute-start | bytes 3932168 | tf_op jit(solution)/shard_map/ppermute | solution.py:22
  62.2 19.1 %collective-permute-start.8 = (bf16[2560,512]{1,0:T(8,128)(2,1)}, bf16[2560,512]{1,0:T(8,128)(2,1)}, u32[]{:S(2)}, u32[]{:S(2)}) collective-permute-start(bf16[2560,512]{1,0:T(8,128)(2,1)} %get-tuple-element.75), channel_id=1, source_target_pairs={{0,32},{1,33},{2,34},{3,35},{4,36},{5,37},{6,38},{7,39},{8,40},{9,... | collective-permute-start | bytes 7864328 | tf_op jit(solution)/shard_map/ppermute | solution.py:22
  87.9 20.4 %collective-permute-start.9 = (f32[256,1024]{1,0:T(8,128)}, f32[256,1024]{1,0:T(8,128)}, u32[]{:S(2)}, u32[]{:S(2)}) collective-permute-start(f32[256,1024]{1,0:T(8,128)} %constant_dynamic-slice_fusion.2), channel_id=1, source_target_pairs={{0,32},{1,33},{2,34},{3,35},{4,36},{5,37},{6,38},{7,39},{8,40},{9,... | collective-permute-start | bytes 3145736 | tf_op jit(solution)/shard_map/ppermute | solution.py:22
  122.8 5.1 %collective-permute-start.17 = (f32[5,256]{1,0:T(8,128)S(1)}, f32[5,256]{1,0:T(8,128)S(1)}, u32[]{:S(2)}, u32[]{:S(2)}) collective-permute-start(f32[5,256]{1,0:T(8,128)S(1)} %stack.43), channel_id=1, source_target_pairs={{0,24},{1,25},{2,26},{3,27},{4,28},{5,29},{6,30},{7,31},{8,16},{9,... | collective-permute-start | bytes 15368 | tf_op jit(solution)/shard_map/ppermute | solution.py:22
  138.4 11.4 %collective-permute-start.20 = (f32[5,256]{1,0:T(8,128)S(1)}, f32[5,256]{1,0:T(8,128)S(1)}, u32[]{:S(2)}, u32[]{:S(2)}) collective-permute-start(f32[5,256]{1,0:T(8,128)S(1)} %stack.46), channel_id=1, source_target_pairs={{0,1},{1,0},{2,3},{3,2},{4,5},{5,4},{6,7},{7,6},{8,9},{9,8},{10,11... | collective-permute-start | bytes 15368 | tf_op jit(solution)/shard_map/ppermute | solution.py:22
  151.2 13.7 %collective-permute-start.21 = (f32[5,256]{1,0:T(8,128)S(1)}, f32[5,256]{1,0:T(8,128)S(1)}, u32[]{:S(2)}, u32[]{:S(2)}) collective-permute-start(f32[5,256]{1,0:T(8,128)S(1)} %stack.47), channel_id=1, source_target_pairs={{0,35},{1,34},{2,33},{3,32},{4,39},{5,38},{6,37},{7,36},{8,43},{9,... | collective-permute-start | bytes 15368 | tf_op jit(solution)/shard_map/ppermute | solution.py:22
  171.7 9.8 %collective-permute-start.28 = (bf16[256,1280]{1,0:T(8,128)(2,1)S(1)}, bf16[256,1280]{1,0:T(8,128)(2,1)S(1)}, u32[]{:S(2)}, u32[]{:S(2)}) collective-permute-start(bf16[256,1280]{1,0:T(8,128)(2,1)S(1)} %convolution_convert_fusion.1), channel_id=1, source_target_pairs={{0,192},{1,193},{2,194},{3,195},{4,196},{5,197},{6,198},{7,199},{8... | collective-permute-start | bytes 1966088 | tf_op jit(solution)/shard_map/ppermute | solution.py:22
  174.2 12.1 %collective-permute-start.24 = (bf16[256,1280]{1,0:T(8,128)(2,1)S(1)}, bf16[256,1280]{1,0:T(8,128)(2,1)S(1)}, u32[]{:S(2)}, u32[]{:S(2)}) collective-permute-start(bf16[256,1280]{1,0:T(8,128)(2,1)S(1)} %convolution_convert_fusion.2), channel_id=1, source_target_pairs={{0,3},{1,2},{2,1},{3,0},{4,7},{5,6},{6,5},{7,4},{8,11},{9,10},{10,... | collective-permute-start | bytes 1966088 | tf_op jit(solution)/shard_map/ppermute | solution.py:22
  183.8 7.2 %collective-permute-start.29 = (bf16[128,1280]{1,0:T(8,128)(2,1)S(1)}, bf16[128,1280]{1,0:T(8,128)(2,1)S(1)}, u32[]{:S(2)}, u32[]{:S(2)}) collective-permute-start(bf16[128,1280]{1,0:T(8,128)(2,1)S(1)} %slice.868), channel_id=1, source_target_pairs={{0,64},{1,65},{2,66},{3,67},{4,68},{5,69},{6,70},{7,71},{8,72},{9,... | collective-permute-start | bytes 983048 | tf_op jit(solution)/shard_map/ppermute | solution.py:22
  188.5 7.2 %collective-permute-start.25 = (bf16[128,1280]{1,0:T(8,128)(2,1)S(1)}, bf16[128,1280]{1,0:T(8,128)(2,1)S(1)}, u32[]{:S(2)}, u32[]{:S(2)}) collective-permute-start(bf16[128,1280]{1,0:T(8,128)(2,1)S(1)} %slice.869), channel_id=1, source_target_pairs={{0,1},{1,0},{2,3},{3,2},{4,5},{5,4},{6,7},{7,6},{8,9},{9,8},{10,11... | collective-permute-start | bytes 983048 | tf_op jit(solution)/shard_map/ppermute | solution.py:22
  191.1 6.0 %collective-permute-start.30 = (bf16[64,1280]{1,0:T(8,128)(2,1)S(1)}, bf16[64,1280]{1,0:T(8,128)(2,1)S(1)}, u32[]{:S(2)}, u32[]{:S(2)}) collective-permute-start(bf16[64,1280]{1,0:T(8,128)(2,1)S(1)} %slice.870), channel_id=1, source_target_pairs={{0,3},{1,2},{2,1},{3,0},{4,7},{5,6},{6,5},{7,4},{8,11},{9,10},{10,... | collective-permute-start | bytes 491528 | tf_op jit(solution)/shard_map/ppermute | solution.py:22
  200.2 5.7 %collective-permute-start.27 = (bf16[32,1280]{1,0:T(8,128)(2,1)S(1)}, bf16[32,1280]{1,0:T(8,128)(2,1)S(1)}, u32[]{:S(2)}, u32[]{:S(2)}) collective-permute-start(bf16[32,1280]{1,0:T(8,128)(2,1)S(1)} %slice.873), channel_id=1, source_target_pairs={{0,64},{1,65},{2,66},{3,67},{4,68},{5,69},{6,70},{7,71},{8,72},{9,... | collective-permute-start | bytes 245768 | tf_op jit(solution)/shard_map/ppermute | solution.py:22
  205.9 6.2 %collective-permute-start.32 = (bf16[16,2560]{1,0:T(8,128)(2,1)S(1)}, bf16[16,2560]{1,0:T(8,128)(2,1)S(1)}, u32[]{:S(2)}, u32[]{:S(2)}) collective-permute-start(bf16[16,2560]{1,0:T(8,128)(2,1)S(1)} %fusion.8), channel_id=1, source_target_pairs={{0,24},{1,25},{2,26},{3,27},{4,28},{5,29},{6,30},{7,31},{8,16},{9,... | collective-permute-start | bytes 245768 | tf_op jit(solution)/shard_map/ppermute | solution.py:22
  216.2 7.9 %collective-permute-start.34 = (bf16[4,2560]{1,0:T(4,128)(2,1)S(1)}, bf16[4,2560]{1,0:T(4,128)(2,1)S(1)}, u32[]{:S(2)}, u32[]{:S(2)}) collective-permute-start(bf16[4,2560]{1,0:T(4,128)(2,1)S(1)} %slice.875), channel_id=1, source_target_pairs={{0,4},{1,5},{2,6},{3,7},{4,0},{5,1},{6,2},{7,3},{8,12},{9,13},{10,... | collective-permute-start | bytes 61448 | tf_op jit(solution)/shard_map/ppermute | solution.py:22
  216.3 11.5 %collective-permute-start.22 = (f32[4]{0:T(128)S(1)}, f32[4]{0:T(128)S(1)}, u32[]{:S(2)}, u32[]{:S(2)}) collective-permute-start(f32[4]{0:T(128)S(1)} %slice.634), channel_id=1, source_target_pairs={{0,32},{1,33},{2,34},{3,35},{4,36},{5,37},{6,38},{7,39},{8,40},{9,... | collective-permute-start | bytes 56 | tf_op jit(solution)/shard_map/ppermute | solution.py:22
  (20 other events, 187.6 us)
